TPU v7x, 32 devices: a whole 2x2x4 slice. The times are simulated.
32 devices in a mesh: grp: 2 (over y), inner: 4 (over x, core), outer: 4 (over z).
Axes of the slice: x: 2, y: 2, z: 4, core: 2. Of those that a mesh axis runs over, the one named last changes fastest.
Arguments:
- queries: bfloat16 [8, 1024, 2048], P(('grp', 'outer'), 'inner'), parts along dimension 0, may hold values from -8 to 8
- keys: bfloat16 [8, 1024, 512], P(('grp', 'outer'), 'inner'), parts along dimension 0, may hold values from -5 to 5
- values: bfloat16 [8, 1024, 512], P(('grp', 'outer'), 'inner'), parts along dimension 0, may hold values from -6 to 6
- out_grad: bfloat16 [8, 1024, 2048], P(('grp', 'outer'), 'inner'), parts along dimension 0, may hold values from -6 to 6
- attn_out: bfloat16 [8, 1024, 2048], P(('grp', 'outer'), 'inner'), parts along dimension 0, may hold values from -6 to 6
- block_mask: int32 [8, 4, 3], P(('grp', 'outer'), 'inner'), parts along dimension 0, may hold values 0 or 1
- scale_exponents: int32 [8, 4, 8], P(('grp', 'outer'), 'inner'), parts along dimension 0, may hold values from -1 to 1
Outputs:
- query_grad: bfloat16 [8, 1024, 2048], P(('grp', 'outer'), 'inner'), parts along dimension 0
- key_grad: bfloat16 [8, 1024, 512], P(('grp', 'outer'), 'inner'), parts along dimension 0
- value_grad: bfloat16 [8, 1024, 512], P(('grp', 'outer'), 'inner'), parts along dimension 0
There are 2 independent parts, one for each index of `grp`. A program takes and returns all parts, laid end to end along the dimension named above; each array names one. Nothing has to cross between parts.
All inputs are finite; a program needn't handle non-finite values. No bound on the sum of `block_mask` on one device may be relied on, other than what follows from the above.
Results may differ from a plain program's by a relative error of at most 0.005.
Values may be sent and summed in bfloat16 or wider, within the bound.
A program may use at most 64 MiB of HBM per device.

v0:
```python
import jax
import jax.numpy as jnp
from jax import lax
from jax.sharding import PartitionSpec as P

HEAD_DIM = 128
STEPS = 4


def shifted(x, axis, by):
    devices = lax.axis_size(axis)
    pairs = [(i, i + by) for i in range(devices) if 0 <= i + by < devices]
    return lax.ppermute(x, axis, pairs)


def from_behind(value, axis, steps):
    count = lax.axis_size(axis)
    pairs = [(source, (source + steps) % count) for source in range(count)]
    return lax.ppermute(value, axis, pairs)


def body(queries, keys, values, out_grad, attn_out, block_mask, scale_exponents):
    length = queries.shape[1]
    kv_width = keys.shape[2]
    kv_count = kv_width // HEAD_DIM
    group_size = queries.shape[2] // kv_width
    score_scale = HEAD_DIM ** (-0.5)
    inner_pos = lax.axis_index("inner")
    outer_pos = lax.axis_index("outer")
    inner_count = lax.axis_size("inner")
    block_index = outer_pos * inner_count + inner_pos
    factors = jnp.exp2(scale_exponents[0, 0].astype(jnp.float32))
    key_factor = jnp.repeat(factors[:kv_count], HEAD_DIM)
    value_factor = jnp.repeat(factors[kv_count:], HEAD_DIM)
    home_pair = jnp.stack(
        [
            (keys[0].astype(jnp.float32) * key_factor).astype(jnp.bfloat16),
            (values[0].astype(jnp.float32) * value_factor).astype(jnp.bfloat16),
        ]
    )
    query_heads = queries[0].reshape(length, kv_count, group_size, HEAD_DIM)
    grad_heads = out_grad[0].reshape(length, kv_count, group_size, HEAD_DIM)
    saved_heads = attn_out[0].reshape(length, kv_count, group_size, HEAD_DIM)
    row_delta = jnp.sum(
        grad_heads.astype(jnp.float32) * saved_heads.astype(jnp.float32), -1
    ).transpose(1, 2, 0)
    positions = jnp.arange(length)
    causal = positions[:, None] >= positions[None, :]

    def is_live(s):
        return (block_index >= s) & (block_mask[0, 0, s - 1] == 1)

    def masked_scores(pair, s):
        key_part = pair[0].reshape(length, kv_count, HEAD_DIM)
        scores = (
            jnp.einsum("tgqd,ugd->gqtu", query_heads, key_part, preferred_element_type=jnp.float32)
            * score_scale
        )
        if s == 0:
            return jnp.where(causal, scores, -1e30)
        return jnp.where(is_live(s), scores, -1e30)

    stored = []
    previous = shifted(home_pair, "outer", 1)
    for s in range(STEPS):
        if s == 0:
            stored.append(home_pair)
        else:
            outgoing = jnp.where(inner_pos >= inner_count - s, previous, home_pair)
            stored.append(from_behind(outgoing, "inner", s))
    first_scores = masked_scores(stored[0], 0)
    row_max = jnp.max(first_scores, -1)
    row_sum = jnp.sum(jnp.exp(first_scores - row_max[..., None]), -1)
    for s in range(1, STEPS):
        fold_pair = stored[s]
        old_max = row_max
        old_sum = row_sum
        fold_scores = masked_scores(fold_pair, s)
        new_max = jnp.maximum(old_max, jnp.max(fold_scores, -1))
        new_sum = old_sum * jnp.exp(old_max - new_max) + jnp.sum(
            jnp.exp(fold_scores - new_max[..., None]), -1
        )
        row_max = new_max
        row_sum = new_sum
    lse = row_max + jnp.log(row_sum)
    query_sum = jnp.zeros((length, kv_count, group_size, HEAD_DIM), jnp.float32)
    own_sum = jnp.zeros((2, length, kv_width), jnp.float32)
    earlier_sum = jnp.zeros((2, length, kv_width), jnp.float32)
    for s in range(STEPS):
        contribution_pair = stored[s]
        contribution_key_part = contribution_pair[0].reshape(length, kv_count, HEAD_DIM)
        value_part = contribution_pair[1].reshape(length, kv_count, HEAD_DIM)
        probs = jnp.exp(masked_scores(contribution_pair, s) - lse[..., None])
        probs_low = probs.astype(jnp.bfloat16)
        dprobs = jnp.einsum(
            "tgqd,ugd->gqtu", grad_heads, value_part, preferred_element_type=jnp.float32
        )
        dscores = (probs * (dprobs - row_delta[..., None])).astype(jnp.bfloat16)
        query_term = (
            jnp.einsum(
                "gqtu,ugd->tgqd", dscores, contribution_key_part, preferred_element_type=jnp.float32
            )
            * score_scale
        )
        key_term = (
            jnp.einsum("gqtu,tgqd->ugd", dscores, query_heads, preferred_element_type=jnp.float32)
            * score_scale
        )
        value_term = jnp.einsum(
            "gqtu,tgqd->ugd", probs_low, grad_heads, preferred_element_type=jnp.float32
        )
        query_term, kv_term = (
            query_term,
            jnp.stack([key_term.reshape(length, kv_width), value_term.reshape(length, kv_width)]),
        )
        query_sum = query_sum + query_term
        if s == 0:
            own_sum = kv_term
        else:
            landed = from_behind(kv_term, "inner", -s)
            wrapped = inner_pos >= inner_count - s
            own_sum = own_sum + jnp.where(wrapped, 0.0, landed)
            earlier_sum = earlier_sum + jnp.where(wrapped, landed, 0.0)
    gradients = own_sum + shifted(earlier_sum, "outer", -1)
    query_grad = query_sum.reshape(1, length, kv_count * group_size * HEAD_DIM).astype(jnp.bfloat16)
    key_grad = (gradients[0] * key_factor).astype(jnp.bfloat16)[None]
    value_grad = (gradients[1] * value_factor).astype(jnp.bfloat16)[None]
    return (query_grad, key_grad, value_grad)


def solution(mesh):
    return jax.shard_map(
        body,
        mesh=mesh,
        in_specs=(
            P(("grp", "outer"), "inner", None),
            P(("grp", "outer"), "inner", None),
            P(("grp", "outer"), "inner", None),
            P(("grp", "outer"), "inner", None),
            P(("grp", "outer"), "inner", None),
            P(("grp", "outer"), "inner", None),
            P(("grp", "outer"), "inner", None),
        ),
        out_specs=(
            P(("grp", "outer"), "inner", None),
            P(("grp", "outer"), "inner", None),
            P(("grp", "outer"), "inner", None),
        ),
        check_vma=False,
    )
```

profile of v0, /device:TPU:0, one launch (start us, length us, event | category | flops | bytes accessed | tf_op | source)
XLA Modules:
  0.0 147.7 jit_solution(10859602335324146184)
XLA Ops:
  0.6 0.7 multiply_exponential_fusion
  1.3 0.1 slice_bitcast_fusion.1
  1.4 1.1 copy.94
  2.5 1.1 copy.97
  3.5 0.1 broadcast_bitcast_fusion
  3.6 0.1 multiply_convert_fusion.3
  3.8 0.1 multiply_convert_fusion.2
  3.9 0.1 pad_maximum_fusion.3
  4.0 5.8 %collective-permute-start = (bf16[2,256,512]{1,2,0:T(8,128)(2,1)S(1)}, bf16[2,256,512]{1,2,0:T(8,128)(2,1)}, u32[]{:S(2)}, u32[]{:S(2)}) collective-permute-start(bf16[2,256,512]{1,2,0:T(8,128)(2,1)S(1)} %pad_maximum_fusion.3), channel_id=1, source_target_pairs={{0,1},{1,2},{2,3},{4,5},{5,6},{6,7},{8,9},{9,10},{10,11},{12,13},{... | collective-permute-start | bytes 1572872 | tf_op jit(solution)/shard_map/ppermute | solution.py:13
  9.7 1.4 fusion.75
  13.0 0.9 copy.104
  14.0 1.8 %reshape_squeeze.35 = bf16[256,4,4,128]{3,2,1,0:T(4,128)(2,1)S(1)} reshape(bf16[1,256,2048]{2,1,0:T(8,128)(2,1)} %param.10) | data formatting | bytes 2097152 | tf_op jit(solution)/shard_map/reshape;squeeze | solution.py:42
  15.7 1.6 %copy.120 = bf16[256,4,4,128]{0,3,2,1:T(8,128)(2,1)} copy(bf16[256,4,4,128]{3,2,1,0:T(4,128)(2,1)S(1)} %reshape_squeeze.35) | data formatting | bytes 2097152 | tf_op jit(solution)/shard_map/reshape;squeeze | solution.py:42
  17.3 1.5 copy.182
  18.8 3.8 %reshape.131 = f32[256,4,4,128]{3,2,1,0:T(4,128)} reshape(bf16[1,256,2048]{2,1,0:T(8,128)(2,1)} %param.11) | data formatting | bytes 3145728 | tf_op jit(solution)/shard_map/convert_element_type | solution.py:45
  22.6 2.9 %fusion.21 = (f32[4,4,256]{2,1,0:T(4,128)S(1)}, f32[4,256,256,4]{2,1,3,0:T(8,128)}) fusion(pred[256,256]{0,1:T(8,128)(4,1)S(1)} %iota_compare_fusion, bf16[256,4,4,128]{0,3,2,1:T(8,128)(2,1)S(1)} %bitcast.260, f32[4]{0:T(128)S(1)} %get-tuple-element.29, bf16[256,4,128]{0,2,1:T(8,128)(2,1)S(1)} %bitcast.269), kind=kOutput, calls=%fused_computation.40 | convolution fusion | flops 271970304 | bytes 5586960 | tf_op jit(solution)/shard_map/tgqd,ugd->gqtu/dot_general | solution.py:56
  25.5 0.0 collective-permute-done
  25.5 2.4 %broadcast_select_fusion.2 = (bf16[2,256,512]{1,2,0:T(8,128)(2,1)}, bf16[2,256,512]{1,2,0:T(8,128)(2,1)}, bf16[2,256,512]{1,2,0:T(8,128)(2,1)}) fusion(bf16[2,256,512]{1,2,0:T(8,128)(2,1)} %collective-permute-done, pred[]{:T(512)S(6)} %ge.41, bf16[1,256,512]{1,2,0:T(8,128)(2,1)S(1)} %multiply_convert_fusion.2, ...), kind=kLoop, calls=%fused_computation.90 | loop fusion | flops 1048576 | bytes 2621443 | tf_op jit(solution)/shard_map/jit(_where)/select_n | solution.py:69
  27.8 1.6 %multiply_reduce_fusion = f32[256,4,4]{2,1,0:T(4,128)S(1)} fusion(f32[256,4,4,128]{3,2,1,0:T(4,128)S(1)} %copy-done.1, bf16[256,4,4,128]{3,2,1,0:T(4,128)(2,1)S(1)} %reshape_squeeze.35), kind=kLoop, calls=%fused_computation.46 | loop fusion | flops 1568768 | bytes 3162112 | tf_op jit(solution)/shard_map/reduce_sum | solution.py:44
  29.5 0.2 copy.106
  29.7 3.1 %exponential_reduce_fusion = f32[4,4,256]{2,1,0:T(4,128)S(1)} fusion(f32[4,256,256,4]{2,1,3,0:T(8,128)} %get-tuple-element.36, f32[4,4,256]{2,1,0:T(4,128)S(1)} %get-tuple-element.35, pred[256,256]{0,1:T(8,128)(4,1)S(1)} %iota_compare_fusion), kind=kLoop, calls=%fused_computation.32 | loop fusion | flops 4190208 | bytes 4292608 | tf_op jit(solution)/shard_map/reduce_sum | solution.py:73
  32.7 2.0 %collective-permute-start.3 = (bf16[2,256,512]{1,2,0:T(8,128)(2,1)}, bf16[2,256,512]{1,2,0:T(8,128)(2,1)S(1)}, u32[]{:S(2)}, u32[]{:S(2)}) collective-permute-start(bf16[2,256,512]{1,2,0:T(8,128)(2,1)} %get-tuple-element.18), channel_id=1, source_target_pairs={{0,12},{4,0},{8,4},{12,8},{1,13},{5,1},{9,5},{13,9},{2,14},{6,2},{... | collective-permute-start | bytes 1572872 | tf_op jit(solution)/shard_map/ppermute | solution.py:19
  34.7 1.5 %collective-permute-start.2 = (bf16[2,256,512]{1,2,0:T(8,128)(2,1)}, bf16[2,256,512]{1,2,0:T(8,128)(2,1)S(1)}, u32[]{:S(2)}, u32[]{:S(2)}) collective-permute-start(bf16[2,256,512]{1,2,0:T(8,128)(2,1)} %get-tuple-element.19), channel_id=1, source_target_pairs={{0,8},{4,12},{8,0},{12,4},{1,9},{5,13},{9,1},{13,5},{2,10},{6,14},... | collective-permute-start | bytes 1572872 | tf_op jit(solution)/shard_map/ppermute | solution.py:19
  36.2 0.4 collective-permute-done.1
  36.7 0.8 bitcast_reduce_fusion.2
  37.5 16.8 %collective-permute-done.2 = bf16[2,256,512]{1,2,0:T(8,128)(2,1)S(1)} collective-permute-done((bf16[2,256,512]{1,2,0:T(8,128)(2,1)}, bf16[2,256,512]{1,2,0:T(8,128)(2,1)S(1)}, u32[]{:S(2)}, u32[]{:S(2)}) %collective-permute-start.2) | collective-permute-done | bytes 524320 | tf_op jit(solution)/shard_map/ppermute | solution.py:19
  54.4 0.8 bitcast_reduce_fusion.1
  55.2 0.8 bitcast_reduce_fusion
  56.1 0.9 fusion.12
  57.0 0.9 fusion.15
  57.8 0.9 fusion.9
  58.8 1.0 fusion.26
  59.8 1.4 fusion.5
  61.1 0.8 fusion.47
  62.0 0.5 fusion.78
  62.4 1.0 fusion.24
  63.4 1.0 fusion.22
  64.4 1.4 fusion.3
  65.8 0.8 fusion.48
  66.6 1.6 %fusion.1 = bf16[4,4,256,256]{2,3,1,0:T(8,128)(2,1)S(1)} fusion(f32[4,256,256,4]{2,1,3,0:T(8,128)S(1)} %get-tuple-element.32, bf16[256,4,128,1]{0,2,3,1:T(8,128)(2,1)S(1)} %bitcast.291, bf16[256,4,4,128]{0,3,2,1:T(8,128)(2,1)S(1)} %copy-done.8, f32[4,4,256]{2,1,0:T(4,128)S(1)} %copy.106, f32[4,4,256]{2,1,0:T(4,128)S(1)} %bitcast.307, pred[]{:T(512)S(6)} %and.16), kind=kOutput, calls=%fused_computation.2 | convolution fusion | flops 274726912 | bytes 7634945 | tf_op jit(solution)/shard_map/tgqd,ugd->gqtu/dot_general | solution.py:95
  68.2 0.8 fusion.49
  69.0 0.1 pad_maximum_fusion.2
  69.1 0.1 collective-permute-start.6
  69.2 0.1 pad_maximum_fusion.1
  69.3 0.7 collective-permute-start.5
  70.0 0.1 pad_maximum_fusion
  70.1 1.5 %collective-permute-start.4 = (f32[2,256,512]{1,2,0:T(8,128)S(1)}, f32[2,256,512]{1,2,0:T(8,128)S(1)}, u32[]{:S(2)}, u32[]{:S(2)}) collective-permute-start(f32[2,256,512]{1,2,0:T(8,128)S(1)} %pad_maximum_fusion), channel_id=1, source_target_pairs={{0,12},{4,0},{8,4},{12,8},{1,13},{5,1},{9,5},{13,9},{2,14},{6,2},{... | collective-permute-start | bytes 3145736 | tf_op jit(solution)/shard_map/ppermute | solution.py:19
  71.6 0.5 fusion.79
  72.0 1.4 fusion.7
  73.5 0.5 fusion.61
  74.0 19.9 %collective-permute-done.6 = f32[2,256,512]{1,2,0:T(8,128)S(1)} collective-permute-done((f32[2,256,512]{1,2,0:T(8,128)S(1)}, f32[2,256,512]{1,2,0:T(8,128)S(1)}, u32[]{:S(2)}, u32[]{:S(2)}) %collective-permute-start.6) | collective-permute-done | bytes 1048608 | tf_op jit(solution)/shard_map/ppermute | solution.py:19
  93.9 1.4 collective-permute-done.5
  95.3 19.9 %collective-permute-done.4 = f32[2,256,512]{1,2,0:T(8,128)S(1)} collective-permute-done((f32[2,256,512]{1,2,0:T(8,128)S(1)}, f32[2,256,512]{1,2,0:T(8,128)S(1)}, u32[]{:S(2)}, u32[]{:S(2)}) %collective-permute-start.4) | collective-permute-done | bytes 1048608 | tf_op jit(solution)/shard_map/ppermute | solution.py:19
  115.3 1.3 select_add_fusion
  116.6 1.3 collective-permute-start.7
  117.9 1.7 %multiply_convert_fusion = bf16[4,128,4,256]{3,1,2,0:T(8,128)(2,1)} fusion(f32[4,128,4,256]{3,1,2,0:T(8,128)S(1)} %fusion.79, f32[4,128,4,256]{3,1,2,0:T(8,128)S(1)} %fusion.61, f32[4,128,4,256]{3,1,2,0:T(8,128)S(1)} %fusion.78, bf16[256,4,128,1]{0,2,3,1:T(8,128)(2,1)S(1)} %bitcast.272, bf16[4,4,256,256]{2,3,1,0:T(8,128)(2,1)S(1)} %fusion.1), kind=kOutput, calls=%fused_computation.45 | convolution fusion | flops 271056896 | bytes 9699328 | tf_op jit(solution)/shard_map/gqtu,ugd->tgqd/dot_general | solution.py:100
  119.6 2.3 %copy.133 = bf16[1,256,2048]{2,1,0:T(8,128)(2,1)} copy(bf16[1,256,2048]{1,2,0:T(8,128)(2,1)} %bitcast.268) | data formatting | bytes 2097152
  121.9 0.8 fusion.46
  122.7 3.7 %fusion.28 = f32[4,256,128,1]{1,2,3,0:T(8,128)S(1)} fusion(bf16[256,4,4,128]{0,3,2,1:T(8,128)(2,1)} %copy.120, f32[4,256,256,4]{2,1,3,0:T(8,128)} %get-tuple-element.36, f32[4,4,256]{2,1,0:T(4,128)S(1)} %bitcast.309, pred[256,256]{0,1:T(8,128)(4,1)S(1)} %iota_compare_fusion), kind=kOutput, calls=%fused_computation.44 | convolution fusion | flops 272629760 | bytes 5849088 | tf_op jit(solution)/shard_map/gqtu,tgqd->ugd/dot_general | solution.py:109
  126.4 17.8 %collective-permute-done.7 = f32[2,256,512]{1,2,0:T(8,128)} collective-permute-done((f32[2,256,512]{1,2,0:T(8,128)}, f32[2,256,512]{1,2,0:T(8,128)}, u32[]{:S(2)}, u32[]{:S(2)}) %collective-permute-start.7) | collective-permute-done | bytes 1048608 | tf_op jit(solution)/shard_map/ppermute | solution.py:13
  144.2 1.6 %fusion.52 = f32[2,256,512]{1,2,0:T(8,128)S(1)} fusion(f32[2,256,512]{1,2,0:T(8,128)} %collective-permute-done.7, f32[1,256,512]{1,2,0:T(8,128)S(1)} %bitcast.286, f32[1,256,512]{1,2,0:T(8,128)S(1)} %bitcast.282, f32[2,256,512]{1,2,0:T(8,128)S(1)} %copy-done.3, f32[2,256,512]{1,2,0:T(8,128)S(1)} %copy-done.5, f32[2,256,512]{1,2,0:T(8,128)S(1)} %copy-done.7, ...), kind=kLoop, calls=%fused_computation.74 | loop fusion | flops 2097152 | bytes 6291459 | tf_op jit(solution)/shard_map/add | solution.py:124
  145.8 0.2 fusion.53
  146.0 0.8 copy.135
  146.9 0.8 copy.134
  (28 shorter events, 0.2 us)
Async XLA Ops:
  4.0 21.5 %collective-permute-start = (bf16[2,256,512]{1,2,0:T(8,128)(2,1)S(1)}, bf16[2,256,512]{1,2,0:T(8,128)(2,1)}, u32[]{:S(2)}, u32[]{:S(2)}) collective-permute-start(bf16[2,256,512]{1,2,0:T(8,128)(2,1)S(1)} %pad_maximum_fusion.3), channel_id=1, source_target_pairs={{0,1},{1,2},{2,3},{4,5},{5,6},{6,7},{8,9},{9,10},{10,11},{12,13},{... | collective-permute-start | bytes 1572872 | tf_op jit(solution)/shard_map/ppermute | solution.py:13
  22.6 5.3 %copy-start.1 = (f32[256,4,4,128]{3,2,1,0:T(4,128)S(1)}, f32[256,4,4,128]{3,2,1,0:T(4,128)}, u32[]{:S(2)}) copy-start(f32[256,4,4,128]{3,2,1,0:T(4,128)} %reshape.131) | copy-start | bytes 6291460
  27.8 8.8 %collective-permute-start.1 = (bf16[2,256,512]{1,2,0:T(8,128)(2,1)}, bf16[2,256,512]{1,2,0:T(8,128)(2,1)S(1)}, u32[]{:S(2)}, u32[]{:S(2)}) collective-permute-start(bf16[2,256,512]{1,2,0:T(8,128)(2,1)} %get-tuple-element.17), channel_id=1, source_target_pairs={{0,4},{4,8},{8,12},{12,0},{1,5},{5,9},{9,13},{13,1},{2,6},{6,10},{... | collective-permute-start | bytes 1572872 | tf_op jit(solution)/shard_map/ppermute | solution.py:19
  32.7 22.4 %collective-permute-start.3 = (bf16[2,256,512]{1,2,0:T(8,128)(2,1)}, bf16[2,256,512]{1,2,0:T(8,128)(2,1)S(1)}, u32[]{:S(2)}, u32[]{:S(2)}) collective-permute-start(bf16[2,256,512]{1,2,0:T(8,128)(2,1)} %get-tuple-element.18), channel_id=1, source_target_pairs={{0,12},{4,0},{8,4},{12,8},{1,13},{5,1},{9,5},{13,9},{2,14},{6,2},{... | collective-permute-start | bytes 1572872 | tf_op jit(solution)/shard_map/ppermute | solution.py:19
  34.7 19.6 %collective-permute-start.2 = (bf16[2,256,512]{1,2,0:T(8,128)(2,1)}, bf16[2,256,512]{1,2,0:T(8,128)(2,1)S(1)}, u32[]{:S(2)}, u32[]{:S(2)}) collective-permute-start(bf16[2,256,512]{1,2,0:T(8,128)(2,1)} %get-tuple-element.19), channel_id=1, source_target_pairs={{0,8},{4,12},{8,0},{12,4},{1,9},{5,13},{9,1},{13,5},{2,10},{6,14},... | collective-permute-start | bytes 1572872 | tf_op jit(solution)/shard_map/ppermute | solution.py:19
  57.0 1.8 %copy-start.8 = (bf16[256,4,4,128]{0,3,2,1:T(8,128)(2,1)S(1)}, bf16[256,4,4,128]{0,3,2,1:T(8,128)(2,1)}, u32[]{:S(2)}) copy-start(bf16[256,4,4,128]{0,3,2,1:T(8,128)(2,1)} %copy.120) | copy-start | bytes 3145732
  69.1 24.8 %collective-permute-start.6 = (f32[2,256,512]{1,2,0:T(8,128)S(1)}, f32[2,256,512]{1,2,0:T(8,128)S(1)}, u32[]{:S(2)}, u32[]{:S(2)}) collective-permute-start(f32[2,256,512]{1,2,0:T(8,128)S(1)} %pad_maximum_fusion.2), channel_id=1, source_target_pairs={{0,4},{4,8},{8,12},{12,0},{1,5},{5,9},{9,13},{13,1},{2,6},{6,10},{... | collective-permute-start | bytes 3145736 | tf_op jit(solution)/shard_map/ppermute | solution.py:19
  69.2 2.8 %copy-start = (f32[4,256,256,4]{2,1,3,0:T(8,128)S(1)}, f32[4,256,256,4]{2,1,3,0:T(8,128)}, u32[]{:S(2)}) copy-start(f32[4,256,256,4]{2,1,3,0:T(8,128)} %get-tuple-element.36) | copy-start | bytes 12582916
  69.2 2.8 %copy-start.9 = (f32[256,4,128]{2,0,1:T(8,128)S(1)}, f32[256,4,128]{2,0,1:T(8,128)}, u32[]{:S(2)}) copy-start(f32[256,4,128]{2,0,1:T(8,128)} %copy.104) | copy-start | bytes 1572868
  69.3 26.1 %collective-permute-start.5 = (f32[2,256,512]{1,2,0:T(8,128)S(1)}, f32[2,256,512]{1,2,0:T(8,128)S(1)}, u32[]{:S(2)}, u32[]{:S(2)}) collective-permute-start(f32[2,256,512]{1,2,0:T(8,128)S(1)} %pad_maximum_fusion.1), channel_id=1, source_target_pairs={{0,8},{4,12},{8,0},{12,4},{1,9},{5,13},{9,1},{13,5},{2,10},{6,14},... | collective-permute-start | bytes 3145736 | tf_op jit(solution)/shard_map/ppermute | solution.py:19
  70.1 45.2 %collective-permute-start.4 = (f32[2,256,512]{1,2,0:T(8,128)S(1)}, f32[2,256,512]{1,2,0:T(8,128)S(1)}, u32[]{:S(2)}, u32[]{:S(2)}) collective-permute-start(f32[2,256,512]{1,2,0:T(8,128)S(1)} %pad_maximum_fusion), channel_id=1, source_target_pairs={{0,12},{4,0},{8,4},{12,8},{1,13},{5,1},{9,5},{13,9},{2,14},{6,2},{... | collective-permute-start | bytes 3145736 | tf_op jit(solution)/shard_map/ppermute | solution.py:19
  93.9 25.7 %copy-start.2 = (f32[2,256,512]{1,2,0:T(8,128)}, f32[2,256,512]{1,2,0:T(8,128)S(1)}, u32[]{:S(2)}) copy-start(f32[2,256,512]{1,2,0:T(8,128)S(1)} %collective-permute-done.6) | copy-start | bytes 3145732
  95.3 24.3 %copy-start.4 = (f32[2,256,512]{1,2,0:T(8,128)}, f32[2,256,512]{1,2,0:T(8,128)S(1)}, u32[]{:S(2)}) copy-start(f32[2,256,512]{1,2,0:T(8,128)S(1)} %collective-permute-done.5) | copy-start | bytes 3145732
  115.3 4.3 %copy-start.6 = (f32[2,256,512]{1,2,0:T(8,128)}, f32[2,256,512]{1,2,0:T(8,128)S(1)}, u32[]{:S(2)}) copy-start(f32[2,256,512]{1,2,0:T(8,128)S(1)} %collective-permute-done.4) | copy-start | bytes 3145732
  116.6 27.6 %collective-permute-start.7 = (f32[2,256,512]{1,2,0:T(8,128)}, f32[2,256,512]{1,2,0:T(8,128)}, u32[]{:S(2)}, u32[]{:S(2)}) collective-permute-start(f32[2,256,512]{1,2,0:T(8,128)} %select_add_fusion), channel_id=1, source_target_pairs={{1,0},{2,1},{3,2},{5,4},{6,5},{7,6},{9,8},{10,9},{11,10},{13,12},{... | collective-permute-start | bytes 3145736 | tf_op jit(solution)/shard_map/ppermute | solution.py:13
  122.7 21.5 %copy-start.3 = (f32[2,256,512]{1,2,0:T(8,128)S(1)}, f32[2,256,512]{1,2,0:T(8,128)}, u32[]{:S(2)}) copy-start(f32[2,256,512]{1,2,0:T(8,128)} %copy-done.2) | copy-start | bytes 3145732
  122.7 21.5 %copy-start.5 = (f32[2,256,512]{1,2,0:T(8,128)S(1)}, f32[2,256,512]{1,2,0:T(8,128)}, u32[]{:S(2)}) copy-start(f32[2,256,512]{1,2,0:T(8,128)} %copy-done.4) | copy-start | bytes 3145732
  122.7 21.5 %copy-start.7 = (f32[2,256,512]{1,2,0:T(8,128)S(1)}, f32[2,256,512]{1,2,0:T(8,128)}, u32[]{:S(2)}) copy-start(f32[2,256,512]{1,2,0:T(8,128)} %copy-done.6) | copy-start | bytes 3145732
where the time goes:
time: 148 us
  waiting for transfers between devices  76.3 us (52%)
  matrix products  24.1 us (16%)
  local copies, waits for them, and re-layouts  17.5 us (12%)
  other arithmetic  14 us (9%)
  starting transfers between devices  12.8 us (9%)
  between operations  2.92 us (2%)
    ppermute x6, waiting for transfers between devices, from_behind(): return lax.ppermute(value, axis, pairs)  58.5 us
    ppermute x2, waiting for transfers between devices, shifted(): return lax.ppermute(x, axis, pairs)  17.8 us
    ppermute x2, starting transfers between devices, shifted(): return lax.ppermute(x, axis, pairs)  7.05 us
    dot_general x4, matrix products, body(): jnp.einsum('gqtu,tgqd->ugd', probs_low, grad_heads, preferred_element_typ...  6.72 us
    unnamed x25, local copies, waits for them, and re-layouts  6.16 us
    ppermute x6, starting transfers between devices, from_behind(): return lax.ppermute(value, axis, pairs)  5.74 us
    dot_general x4, matrix products, body(): jnp.einsum('tgqd,ugd->gqtu', grad_heads, value_part, preferred_element_ty...  5.72 us
    dot_general x4, matrix products, masked_scores(): jnp.einsum('tgqd,ugd->gqtu', query_heads, key_part, preferred_element_typ...  5.32 us
  transfers between devices with their start and end apart: 8, of which 6 were waited for; matrix products, arithmetic and copies ran while one was open for 21% of the time, Pallas kernels for 0%

commit v1 on v0

v1 whole, which is shorter than its diff:
```python
import functools

import jax
import jax.numpy as jnp
from jax import lax
from jax.experimental import pallas as pl
from jax.experimental.pallas import tpu as pltpu
from jax.sharding import PartitionSpec as P

HEAD_DIM = 128
STEPS = 4
NT = (((1,), (1,)), ((), ()))
NN = (((1,), (0,)), ((), ()))
LOG2E = 1.4426950408889634


def dot(a, b, dims):
    return lax.dot_general(a, b, dims, preferred_element_type=jnp.float32)


def power(e):
    return jnp.where(e > 0, 2.0, jnp.where(e < 0, 0.5, 1.0)).astype(jnp.float32)


def kernel(
    inner_count, outer_count, kv_count, group_size, length,
    mask_ref, exp_ref, k_ref, v_ref, q_ref, do_ref, o_ref,
    dq_ref, dk_ref, dv_ref,
    kv, kt, delta, acc, own, part, comb, rin,
    fwd_send, fwd_recv, bwd_send, bwd_recv,
):
    scale = HEAD_DIM ** (-0.5)
    b = lax.axis_index("outer") * inner_count + lax.axis_index("inner")
    c = lax.rem(lax.axis_index("inner"), 2)
    total = inner_count * outer_count
    partner = b + 1 - 2 * c

    def device(t):
        return {"outer": t // inner_count, "inner": lax.rem(t, inner_count)}

    def remote(src, dst, send, recv, t):
        return pltpu.make_async_remote_copy(
            src_ref=src, dst_ref=dst, send_sem=send, recv_sem=recv,
            device_id=device(t), device_id_type=pl.DeviceIdType.MESH,
        )

    far_up = b + 3 * c
    neighbours = [
        (partner, None),
        (b + 2, b + 2 < total),
        (b - 2, b >= 2),
        (b - 3 + 6 * c, jnp.logical_and(b - 3 + 6 * c >= 0, b - 3 + 6 * c < total)),
    ]
    barrier = pltpu.get_barrier_semaphore()

    def guarded(cond, fn):
        if cond is None:
            fn()
        else:
            pl.when(cond)(fn)

    for t, cond in neighbours:
        guarded(cond, lambda t=t: pl.semaphore_signal(
            barrier, inc=1, device_id=device(t), device_id_type=pl.DeviceIdType.MESH))

    for g in range(kv_count):
        cols = pl.ds(g * HEAD_DIM, HEAD_DIM)
        kf = power(exp_ref[0, 0, g])
        vf = power(exp_ref[0, 0, kv_count + g])
        kv[g, 0, 0] = (k_ref[0, :, cols].astype(jnp.float32) * kf).astype(jnp.bfloat16)
        kv[g, 1, 0] = (v_ref[0, :, cols].astype(jnp.float32) * vf).astype(jnp.bfloat16)

    pl.semaphore_wait(barrier, sum(
        (1 if cond is None else cond.astype(jnp.int32)) for _, cond in neighbours))

    def fwd_far(g):
        return remote(kv.at[g, :, 0], kv.at[g, :, 2], fwd_send.at[0, g], fwd_recv.at[2, g], b + 2)

    def fwd_second(g):
        slot = 1 + 2 * c
        return remote(kv.at[g, :, 0], kv.at[g, :, slot], fwd_send.at[1, g], fwd_recv.at[slot, g], b + 1 + 2 * c)

    def fwd_pass(g):
        slot = 3 - 2 * c
        return remote(kv.at[g, :, 2], kv.at[g, :, slot], fwd_send.at[2, g], fwd_recv.at[slot, g], partner)

    def fwd_wait(s, g):
        remote(kv.at[g, :, s], kv.at[g, :, s], fwd_send.at[0, g], fwd_recv.at[s, g], partner).wait_recv()

    has_far = b + 2 < total
    has_second = b + 1 + 2 * c < total
    has_prev = b >= 2
    has_back = b - 3 + 2 * c >= 0
    has_final = b + 1 + 2 * c < total

    for g in range(kv_count):
        pl.when(has_far)(lambda g=g: fwd_far(g).start())
        pl.when(has_second)(lambda g=g: fwd_second(g).start())

    for s in range(1, STEPS):
        @pl.when(b < s)
        def _():
            for g in range(kv_count):
                for i in range(2):
                    kv[g, i, s] = jnp.zeros((length, HEAD_DIM), jnp.bfloat16)

    heads = kv_count * group_size

    @pl.loop(0, heads)
    def _(h):
        cols = pl.ds(pl.multiple_of(h * HEAD_DIM, HEAD_DIM), HEAD_DIM)
        prod = do_ref[0, :, cols].astype(jnp.float32) * o_ref[0, :, cols].astype(jnp.float32)
        high = prod.astype(jnp.bfloat16)
        low = (prod - high.astype(jnp.float32)).astype(jnp.bfloat16)
        ones = jnp.ones((16, HEAD_DIM), jnp.bfloat16)
        delta[h] = dot(ones, high, NT) + dot(ones, low, NT)

    bias = [None] + [
        jnp.where(jnp.logical_and(b >= s, mask_ref[0, 0, s - 1] == 1), 0.0, -1e30).astype(jnp.float32)
        for s in range(1, STEPS)
    ]

    def compute(g, first, count):
        @pl.loop(first, first + count)
        def _(j):
            h = g * group_size + j
            cols = pl.ds(pl.multiple_of(h * HEAD_DIM, HEAD_DIM), HEAD_DIM)
            qh = q_ref[0, :, cols]
            doh = do_ref[0, :, cols]
            scores = []
            top = None
            for s in range(STEPS):
                x = dot(kv[g, 0, s], qh, NT)
                if s == 0:
                    u = lax.broadcasted_iota(jnp.int32, (length, length), 0)
                    t = lax.broadcasted_iota(jnp.int32, (length, length), 1)
                    x = jnp.where(u <= t, x, -1e30)
                else:
                    x = x + bias[s]
                scores.append(x)
                m = jnp.max(x, 0, keepdims=True)
                top = m if top is None else jnp.maximum(top, m)
            top = top * (scale * LOG2E)
            exps = []
            norm = None
            for s in range(STEPS):
                e = jnp.exp2(scores[s] * (scale * LOG2E) - top)
                exps.append(e)
                n = jnp.sum(e, 0, keepdims=True)
                norm = n if norm is None else norm + n
            inv = 1.0 / norm
            d = delta[h, 0:1, :]
            dqt = None
            for s in range(STEPS):
                p = exps[s] * inv
                dp = dot(kv[g, 1, s], doh, NT)
                ds = (p * (dp - d)).astype(jnp.bfloat16)
                term = dot(kt[:, s * length:(s + 1) * length], ds, NN)
                dqt = term if dqt is None else dqt + term
                acc[0, s] += dot(ds, qh, NN)
                acc[1, s] += dot(p.astype(jnp.bfloat16), doh, NN)
            dq_ref[0, :, cols] = (dqt.T * scale).astype(jnp.bfloat16)

    def bwd_combine(g):
        return remote(part.at[g, 2 * c], rin.at[g, 0], bwd_send.at[0, g], bwd_recv.at[0, g], partner)

    def bwd_far(g):
        return remote(comb.at[g], rin.at[g, 1], bwd_send.at[1, g], bwd_recv.at[1, g], b - 2)

    def bwd_second(g):
        return remote(part.at[g, 2 - 2 * c], rin.at[g, 2], bwd_send.at[2, g], bwd_recv.at[2, g], b - 3 + 2 * c)

    def bwd_wait(slot, g):
        remote(rin.at[g, slot], rin.at[g, slot], bwd_send.at[0, g], bwd_recv.at[slot, g], partner).wait_recv()

    def take(g):
        @pl.when(has_prev)
        def _():
            bwd_wait(0, g)
            comb[g] = (part[g, 1].astype(jnp.float32) + rin[g, 0].astype(jnp.float32)).astype(jnp.bfloat16)
            bwd_far(g).start()

    def pass_on(g):
        @pl.when(has_prev)
        def _():
            fwd_wait(2, g)
            fwd_pass(g).start()

    half = group_size // 2
    pass_on(0)
    for g in range(kv_count):
        pl.when(b >= 1)(lambda g=g: fwd_wait(1, g))
        pl.when(b >= 3)(lambda g=g: fwd_wait(3, g))
        for s in range(STEPS):
            kt[:, s * length:(s + 1) * length] = kv[g, 0, s].T
        acc[...] = jnp.zeros_like(acc)
        compute(g, 0, half)
        if g + 1 < kv_count:
            pass_on(g + 1)
        if g > 0:
            take(g - 1)
        compute(g, half, group_size - half)
        own[g] = acc[:, 0]
        for s in range(1, STEPS):
            part[g, s - 1] = acc[:, s].astype(jnp.bfloat16)
        pl.when(has_prev)(lambda g=g: bwd_combine(g).start())
        pl.when(has_back)(lambda g=g: bwd_second(g).start())
    take(kv_count - 1)

    for g in range(kv_count):
        @pl.when(has_far)
        def _():
            bwd_wait(1, g)
            own[g] += rin[g, 1].astype(jnp.float32)

        @pl.when(has_final)
        def _():
            bwd_wait(2, g)
            own[g] += rin[g, 2].astype(jnp.float32)

        cols = pl.ds(g * HEAD_DIM, HEAD_DIM)
        kf = power(exp_ref[0, 0, g]) * scale
        vf = power(exp_ref[0, 0, kv_count + g])
        dk_ref[0, :, cols] = (own[g, 0] * kf).astype(jnp.bfloat16)
        dv_ref[0, :, cols] = (own[g, 1] * vf).astype(jnp.bfloat16)

    for g in range(kv_count):
        @pl.when(has_far)
        def _():
            fwd_far(g).wait_send()

        @pl.when(has_second)
        def _():
            fwd_second(g).wait_send()

        @pl.when(has_prev)
        def _():
            fwd_pass(g).wait_send()
            bwd_combine(g).wait_send()
            bwd_far(g).wait_send()

        @pl.when(has_back)
        def _():
            bwd_second(g).wait_send()


def body(mesh, queries, keys, values, out_grad, attn_out, block_mask, scale_exponents):
    length = queries.shape[1]
    kv_width = keys.shape[2]
    kv_count = kv_width // HEAD_DIM
    group_size = queries.shape[2] // kv_width
    heads = kv_count * group_size
    bf16, f32 = jnp.bfloat16, jnp.float32
    vmem = pl.BlockSpec(memory_space=pltpu.VMEM)
    smem = pl.BlockSpec(memory_space=pltpu.SMEM)
    block = (length, HEAD_DIM)
    return pl.pallas_call(
        functools.partial(
            kernel, mesh.shape["inner"], mesh.shape["outer"], kv_count, group_size, length
        ),
        out_shape=(
            jax.ShapeDtypeStruct(queries.shape, bf16),
            jax.ShapeDtypeStruct(keys.shape, bf16),
            jax.ShapeDtypeStruct(values.shape, bf16),
        ),
        in_specs=[smem, smem] + [vmem] * 5,
        out_specs=(vmem, vmem, vmem),
        scratch_shapes=[
            pltpu.VMEM((kv_count, 2, STEPS) + block, bf16),
            pltpu.VMEM((HEAD_DIM, STEPS * length), bf16),
            pltpu.VMEM((heads, 16, length), f32),
            pltpu.VMEM((2, STEPS) + block, f32),
            pltpu.VMEM((kv_count, 2) + block, f32),
            pltpu.VMEM((kv_count, STEPS - 1, 2) + block, bf16),
            pltpu.VMEM((kv_count, 2) + block, bf16),
            pltpu.VMEM((kv_count, 3, 2) + block, bf16),
            pltpu.SemaphoreType.DMA((3, kv_count)),
            pltpu.SemaphoreType.DMA((STEPS, kv_count)),
            pltpu.SemaphoreType.DMA((3, kv_count)),
            pltpu.SemaphoreType.DMA((3, kv_count)),
        ],
        compiler_params=pltpu.CompilerParams(
            collective_id=0, has_side_effects=True, vmem_limit_bytes=48 * 1024 * 1024
        ),
    )(block_mask, scale_exponents, keys, values, queries, out_grad, attn_out)


def solution(mesh):
    spec = P(("grp", "outer"), "inner", None)
    return jax.shard_map(
        functools.partial(body, mesh),
        mesh=mesh,
        in_specs=(spec,) * 7,
        out_specs=(spec,) * 3,
        check_vma=False,
    )
```

time: 148 us -> 49.4 us (0.33)
  waiting for transfers between devices: 76.3 us -> 0 us
  Pallas kernels: 0 us -> 39 us
  matrix products: 24.1 us -> 0 us
  other arithmetic: 14 us -> 0 us
  starting transfers between devices: 12.8 us -> 0 us
  local copies, waits for them, and re-layouts: 17.5 us -> 9.25 us
  between operations: 2.92 us -> 0.66 us
    ppermute x8 -> x0, waiting for transfers between devices: 76.3 us -> none  [the longest x6 58.5 us: from_behind(): return lax.ppermute(value, axis, pairs)]
    pallas_call x0 -> x1, Pallas kernels: none -> 39 us  [body(): pl.pallas_call(functools.partial(kernel, mesh.shape['inner'], mesh.shape[...]
    dot_general x20 -> x0, matrix products: 24.1 us -> none  [the longest x4 6.72 us: body(): jnp.einsum('gqtu,tgqd->ugd', probs_low, grad_heads, preferred_element_typ...]
    ppermute x8 -> x0, starting transfers between devices: 12.8 us -> none  [the longest x2 7.05 us: shifted(): return lax.ppermute(x, axis, pairs)]
    reduce_sum x5 -> x0, other arithmetic: 7.33 us -> none  [the longest x1 3.07 us: body(): row_sum = jnp.sum(jnp.exp(first_scores - row_max[..., None]), -1)]
    another operation x3 -> x0, local copies, waits for them, and re-layouts: 4.84 us -> none  [the longest x2 3.37 us: body(): grad_heads = out_grad[0].reshape(length, kv_count, group_size, HEAD_DIM)]
    convert_element_type x2 -> x0, local copies, waits for them, and re-layouts: 4.69 us -> none  [the longest x1 3.78 us: body(): saved_heads.astype(jnp.float32)]
    unnamed x25 -> x17, local copies, waits for them, and re-layouts: 6.16 us -> 9.25 us
  transfers between devices with their start and end apart: 8 -> 0, of which waited for: 6 -> 0; matrix products, arithmetic and copies ran while one was open for 21% -> 0% of each run, Pallas kernels for 0% -> 0%
where the time goes in v1:
time: 49.4 us; the launch traced here: 48.9 us
  Pallas kernels  39 us (79%)
  local copies, waits for them, and re-layouts  9.25 us (19%)
  between operations  0.66 us (1%)
    pallas_call x1, Pallas kernels, body(): pl.pallas_call(functools.partial(kernel, mesh.shape['inner'], mesh.shape[...  39 us
    unnamed x17, local copies, waits for them, and re-layouts  9.25 us

profile of v1, /device:TPU:0, one launch (start us, length us, event | category | flops | bytes accessed | tf_op | source)
XLA Modules:
  0.0 48.9 jit_solution(12324288050758377116)
XLA Ops:
  0.6 0.0 copy-start
  0.6 1.2 %copy-done = bf16[1,256,2048]{2,1,0:T(8,128)(2,1)S(1)} copy-done((bf16[1,256,2048]{2,1,0:T(8,128)(2,1)S(1)}, bf16[1,256,2048]{2,1,0:T(8,128)(2,1)}, u32[]{:S(2)}) %copy-start) | copy-done | bytes 1048600
  1.9 0.0 copy-start.1
  1.9 1.2 %copy-done.1 = bf16[1,256,2048]{2,1,0:T(8,128)(2,1)S(1)} copy-done((bf16[1,256,2048]{2,1,0:T(8,128)(2,1)S(1)}, bf16[1,256,2048]{2,1,0:T(8,128)(2,1)}, u32[]{:S(2)}) %copy-start.1) | copy-done | bytes 1048600
  3.1 0.0 copy-start.2
  3.1 1.2 %copy-done.2 = bf16[1,256,2048]{2,1,0:T(8,128)(2,1)S(1)} copy-done((bf16[1,256,2048]{2,1,0:T(8,128)(2,1)S(1)}, bf16[1,256,2048]{2,1,0:T(8,128)(2,1)}, u32[]{:S(2)}) %copy-start.2) | copy-done | bytes 1048600
  4.3 0.0 copy-start.3
  4.3 0.9 %copy-done.3 = bf16[1,256,512]{2,1,0:T(8,128)(2,1)S(1)} copy-done((bf16[1,256,512]{2,1,0:T(8,128)(2,1)S(1)}, bf16[1,256,512]{2,1,0:T(8,128)(2,1)}, u32[]{:S(2)}) %copy-start.3) | copy-done | bytes 262168
  5.3 0.0 copy-start.4
  5.3 0.9 %copy-done.4 = bf16[1,256,512]{2,1,0:T(8,128)(2,1)S(1)} copy-done((bf16[1,256,512]{2,1,0:T(8,128)(2,1)S(1)}, bf16[1,256,512]{2,1,0:T(8,128)(2,1)}, u32[]{:S(2)}) %copy-start.4) | copy-done | bytes 262168
  6.2 0.0 copy-start.5
  6.2 0.7 %copy-done.5 = s32[1,1,3]{2,1,0:T(1,128)S(1)} copy-done((s32[1,1,3]{2,1,0:T(1,128)S(1)}, s32[1,1,3]{2,1,0:T(1,128)}, u32[]{:S(2)}) %copy-start.5) | copy-done | bytes 36
  6.9 0.0 copy-start.6
  6.9 0.7 %copy-done.6 = s32[1,1,8]{2,1,0:T(1,128)S(1)} copy-done((s32[1,1,8]{2,1,0:T(1,128)S(1)}, s32[1,1,8]{2,1,0:T(1,128)}, u32[]{:S(2)}) %copy-start.6) | copy-done | bytes 56
  7.5 39.0 %shard_map.94 = (bf16[1,256,2048]{2,1,0:T(8,128)(2,1)S(1)}, bf16[1,256,512]{2,1,0:T(8,128)(2,1)S(1)}, bf16[1,256,512]{2,1,0:T(8,128)(2,1)S(1)}) custom-call(s32[1,1,3]{2,1,0:T(1,128)S(1)} %copy-done.5, s32[1,1,8]{2,1,0:T(1,128)S(1)} %copy-done.6, bf16[1,256,512]{2,1,0:T(8,128)(2,1)S(1)} %copy-done.3, bf16[1,256,512]{2,1,0:T(8,128)(2,1)S(1)} %copy-done.4, ...), custom_call_target="tpu_custom_call" | custom-call | tf_op jit(solution)/shard_map/pallas_call | solution.py:257
  46.5 1.0 %copy.13 = bf16[1,256,2048]{2,1,0:T(8,128)(2,1)} copy(bf16[1,256,2048]{2,1,0:T(8,128)(2,1)S(1)} %get-tuple-element.6) | data formatting | bytes 2097152
  47.5 0.7 %copy.14 = bf16[1,256,512]{2,1,0:T(8,128)(2,1)} copy(bf16[1,256,512]{2,1,0:T(8,128)(2,1)S(1)} %get-tuple-element.7) | data formatting | bytes 524288
  48.2 0.7 %copy.15 = bf16[1,256,512]{2,1,0:T(8,128)(2,1)} copy(bf16[1,256,512]{2,1,0:T(8,128)(2,1)S(1)} %get-tuple-element.8) | data formatting | bytes 524288
Async XLA Ops:
  0.6 1.2 %copy-start = (bf16[1,256,2048]{2,1,0:T(8,128)(2,1)S(1)}, bf16[1,256,2048]{2,1,0:T(8,128)(2,1)}, u32[]{:S(2)}) copy-start(bf16[1,256,2048]{2,1,0:T(8,128)(2,1)} %q_ref.1) | copy-start | bytes 3145732
  1.9 1.2 %copy-start.1 = (bf16[1,256,2048]{2,1,0:T(8,128)(2,1)S(1)}, bf16[1,256,2048]{2,1,0:T(8,128)(2,1)}, u32[]{:S(2)}) copy-start(bf16[1,256,2048]{2,1,0:T(8,128)(2,1)} %do_ref.1) | copy-start | bytes 3145732
  3.1 1.2 %copy-start.2 = (bf16[1,256,2048]{2,1,0:T(8,128)(2,1)S(1)}, bf16[1,256,2048]{2,1,0:T(8,128)(2,1)}, u32[]{:S(2)}) copy-start(bf16[1,256,2048]{2,1,0:T(8,128)(2,1)} %o_ref.1) | copy-start | bytes 3145732
  4.3 0.9 %copy-start.3 = (bf16[1,256,512]{2,1,0:T(8,128)(2,1)S(1)}, bf16[1,256,512]{2,1,0:T(8,128)(2,1)}, u32[]{:S(2)}) copy-start(bf16[1,256,512]{2,1,0:T(8,128)(2,1)} %k_ref.1) | copy-start | bytes 786436
  5.3 0.9 %copy-start.4 = (bf16[1,256,512]{2,1,0:T(8,128)(2,1)S(1)}, bf16[1,256,512]{2,1,0:T(8,128)(2,1)}, u32[]{:S(2)}) copy-start(bf16[1,256,512]{2,1,0:T(8,128)(2,1)} %v_ref.1) | copy-start | bytes 786436
  6.2 0.7 %copy-start.5 = (s32[1,1,3]{2,1,0:T(1,128)S(1)}, s32[1,1,3]{2,1,0:T(1,128)}, u32[]{:S(2)}) copy-start(s32[1,1,3]{2,1,0:T(1,128)} %mask_ref.1) | copy-start | bytes 40
  6.9 0.7 %copy-start.6 = (s32[1,1,8]{2,1,0:T(1,128)S(1)}, s32[1,1,8]{2,1,0:T(1,128)}, u32[]{:S(2)}) copy-start(s32[1,1,8]{2,1,0:T(1,128)} %exp_ref.1) | copy-start | bytes 100

commit v2 on v1

--- a/solution.py
+++ b/solution.py
@@ -24,11 +24,17 @@
 
 def kernel(
     inner_count, outer_count, kv_count, group_size, length,
-    mask_ref, exp_ref, k_ref, v_ref, q_ref, do_ref, o_ref,
-    dq_ref, dk_ref, dv_ref,
-    kv, kt, delta, acc, own, part, comb, rin,
-    fwd_send, fwd_recv, bwd_send, bwd_recv,
+    *refs,
 ):
+    sources = refs[:7]
+    dq_ref, dk_ref, dv_ref = refs[7:10]
+    kv, kt, delta, weights, tall, own, part, comb, rin = refs[10:19]
+    fwd_send, fwd_recv, bwd_send, bwd_recv, load_sem = refs[19:24]
+    staged = refs[24:]
+    mask_ref, exp_ref, k_ref, v_ref, q_ref, do_ref, o_ref = staged
+    loads = [pltpu.make_async_copy(a, z, load_sem.at[i]) for i, (a, z) in enumerate(zip(sources, staged))]
+    for load in loads:
+        load.start()
     scale = HEAD_DIM ** (-0.5)
     b = lax.axis_index("outer") * inner_count + lax.axis_index("inner")
     c = lax.rem(lax.axis_index("inner"), 2)
@@ -44,7 +50,6 @@
             device_id=device(t), device_id_type=pl.DeviceIdType.MESH,
         )
 
-    far_up = b + 3 * c
     neighbours = [
         (partner, None),
         (b + 2, b + 2 < total),
@@ -63,10 +68,12 @@
         guarded(cond, lambda t=t: pl.semaphore_signal(
             barrier, inc=1, device_id=device(t), device_id_type=pl.DeviceIdType.MESH))
 
+    for load in loads[:4]:
+        load.wait()
     for g in range(kv_count):
         cols = pl.ds(g * HEAD_DIM, HEAD_DIM)
-        kf = power(exp_ref[0, 0, g])
-        vf = power(exp_ref[0, 0, kv_count + g])
+        kf = power(exp_ref[0, :, g:g + 1])
+        vf = power(exp_ref[0, :, kv_count + g:kv_count + g + 1])
         kv[g, 0, 0] = (k_ref[0, :, cols].astype(jnp.float32) * kf).astype(jnp.bfloat16)
         kv[g, 1, 0] = (v_ref[0, :, cols].astype(jnp.float32) * vf).astype(jnp.bfloat16)
 
@@ -93,9 +100,11 @@
     has_back = b - 3 + 2 * c >= 0
     has_final = b + 1 + 2 * c < total
 
-    for g in range(kv_count):
-        pl.when(has_far)(lambda g=g: fwd_far(g).start())
-        pl.when(has_second)(lambda g=g: fwd_second(g).start())
+    def send(g):
+        pl.when(has_far)(lambda: fwd_far(g).start())
+        pl.when(has_second)(lambda: fwd_second(g).start())
+
+    send(0)
 
     for s in range(1, STEPS):
         @pl.when(b < s)
@@ -105,6 +114,8 @@
                     kv[g, i, s] = jnp.zeros((length, HEAD_DIM), jnp.bfloat16)
 
     heads = kv_count * group_size
+    for load in loads[4:]:
+        load.wait()
 
     @pl.loop(0, heads)
     def _(h):
@@ -116,17 +127,21 @@
         delta[h] = dot(ones, high, NT) + dot(ones, low, NT)
 
     bias = [None] + [
-        jnp.where(jnp.logical_and(b >= s, mask_ref[0, 0, s - 1] == 1), 0.0, -1e30).astype(jnp.float32)
+        jnp.where(mask_ref[0, :, s - 1:s] == 1, 0.0, -1e30).astype(jnp.float32)
+        + jnp.where(b >= s, 0.0, -1e30).astype(jnp.float32)
         for s in range(1, STEPS)
     ]
 
     def compute(g, first, count):
-        @pl.loop(first, first + count)
+        @pl.loop(first, first + count, unroll=2)
         def _(j):
             h = g * group_size + j
             cols = pl.ds(pl.multiple_of(h * HEAD_DIM, HEAD_DIM), HEAD_DIM)
             qh = q_ref[0, :, cols]
             doh = do_ref[0, :, cols]
+            rows = pl.ds(pl.multiple_of(j * length, length), length)
+            tall[0, rows, :] = qh
+            tall[1, rows, :] = doh
             scores = []
             top = None
             for s in range(STEPS):
@@ -157,8 +172,9 @@
                 ds = (p * (dp - d)).astype(jnp.bfloat16)
                 term = dot(kt[:, s * length:(s + 1) * length], ds, NN)
                 dqt = term if dqt is None else dqt + term
-                acc[0, s] += dot(ds, qh, NN)
-                acc[1, s] += dot(p.astype(jnp.bfloat16), doh, NN)
+                wide = pl.ds(pl.multiple_of(j * length, length), length)
+                weights[0, s, :, wide] = ds
+                weights[1, s, :, wide] = p.astype(jnp.bfloat16)
             dq_ref[0, :, cols] = (dqt.T * scale).astype(jnp.bfloat16)
 
     def bwd_combine(g):
@@ -187,22 +203,28 @@
             fwd_pass(g).start()
 
     half = group_size // 2
+    send(1)
     pass_on(0)
+    for g in range(2, kv_count):
+        send(g)
     for g in range(kv_count):
         pl.when(b >= 1)(lambda g=g: fwd_wait(1, g))
         pl.when(b >= 3)(lambda g=g: fwd_wait(3, g))
         for s in range(STEPS):
             kt[:, s * length:(s + 1) * length] = kv[g, 0, s].T
-        acc[...] = jnp.zeros_like(acc)
         compute(g, 0, half)
         if g + 1 < kv_count:
             pass_on(g + 1)
         if g > 0:
             take(g - 1)
         compute(g, half, group_size - half)
-        own[g] = acc[:, 0]
-        for s in range(1, STEPS):
-            part[g, s - 1] = acc[:, s].astype(jnp.bfloat16)
+        for s in (3, 1, 2, 0):
+            for i in range(2):
+                x = dot(weights[i, s], tall[i], NN)
+                if s == 0:
+                    own[g, i] = x
+                else:
+                    part[g, s - 1, i] = x.astype(jnp.bfloat16)
         pl.when(has_prev)(lambda g=g: bwd_combine(g).start())
         pl.when(has_back)(lambda g=g: bwd_second(g).start())
     take(kv_count - 1)
@@ -219,8 +241,8 @@
             own[g] += rin[g, 2].astype(jnp.float32)
 
         cols = pl.ds(g * HEAD_DIM, HEAD_DIM)
-        kf = power(exp_ref[0, 0, g]) * scale
-        vf = power(exp_ref[0, 0, kv_count + g])
+        kf = power(exp_ref[0, :, g:g + 1]) * scale
+        vf = power(exp_ref[0, :, kv_count + g:kv_count + g + 1])
         dk_ref[0, :, cols] = (own[g, 0] * kf).astype(jnp.bfloat16)
         dv_ref[0, :, cols] = (own[g, 1] * vf).astype(jnp.bfloat16)
 
@@ -242,6 +264,15 @@
         @pl.when(has_back)
         def _():
             bwd_second(g).wait_send()
+
+
+def write_out(*refs):
+    sems = refs[6]
+    copies = [pltpu.make_async_copy(refs[i], refs[3 + i], sems.at[i]) for i in range(3)]
+    for copy in copies:
+        copy.start()
+    for copy in copies:
+        copy.wait()
 
 
 def body(mesh, queries, keys, values, out_grad, attn_out, block_mask, scale_exponents):
@@ -252,9 +283,10 @@
     heads = kv_count * group_size
     bf16, f32 = jnp.bfloat16, jnp.float32
     vmem = pl.BlockSpec(memory_space=pltpu.VMEM)
-    smem = pl.BlockSpec(memory_space=pltpu.SMEM)
+    anywhere = pl.BlockSpec(memory_space=pl.ANY)
+    arguments = (block_mask, scale_exponents, keys, values, queries, out_grad, attn_out)
     block = (length, HEAD_DIM)
-    return pl.pallas_call(
+    grads = pl.pallas_call(
         functools.partial(
             kernel, mesh.shape["inner"], mesh.shape["outer"], kv_count, group_size, length
         ),
@@ -263,13 +295,14 @@
             jax.ShapeDtypeStruct(keys.shape, bf16),
             jax.ShapeDtypeStruct(values.shape, bf16),
         ),
-        in_specs=[smem, smem] + [vmem] * 5,
+        in_specs=[pl.BlockSpec(memory_space=pltpu.HBM)] * 7,
         out_specs=(vmem, vmem, vmem),
         scratch_shapes=[
             pltpu.VMEM((kv_count, 2, STEPS) + block, bf16),
             pltpu.VMEM((HEAD_DIM, STEPS * length), bf16),
             pltpu.VMEM((heads, 16, length), f32),
-            pltpu.VMEM((2, STEPS) + block, f32),
+            pltpu.VMEM((2, STEPS, length, group_size * length), bf16),
+            pltpu.VMEM((2, group_size * length, HEAD_DIM), bf16),
             pltpu.VMEM((kv_count, 2) + block, f32),
             pltpu.VMEM((kv_count, STEPS - 1, 2) + block, bf16),
             pltpu.VMEM((kv_count, 2) + block, bf16),
@@ -278,11 +311,20 @@
             pltpu.SemaphoreType.DMA((STEPS, kv_count)),
             pltpu.SemaphoreType.DMA((3, kv_count)),
             pltpu.SemaphoreType.DMA((3, kv_count)),
-        ],
+            pltpu.SemaphoreType.DMA((7,)),
+        ] + [pltpu.VMEM(x.shape, x.dtype) for x in arguments],
         compiler_params=pltpu.CompilerParams(
-            collective_id=0, has_side_effects=True, vmem_limit_bytes=48 * 1024 * 1024
+            collective_id=0, has_side_effects=True, vmem_limit_bytes=63 * 1024 * 1024
         ),
-    )(block_mask, scale_exponents, keys, values, queries, out_grad, attn_out)
+    )(*arguments)
+    return pl.pallas_call(
+        write_out,
+        out_shape=tuple(jax.ShapeDtypeStruct(x.shape, x.dtype) for x in grads),
+        in_specs=[anywhere] * 3,
+        out_specs=(anywhere,) * 3,
+        scratch_shapes=[pltpu.SemaphoreType.DMA((3,))],
+        compiler_params=pltpu.CompilerParams(vmem_limit_bytes=63 * 1024 * 1024),
+    )(*grads)
 
 
 def solution(mesh):

time: 49.4 us -> 87.8 us (1.78)
  Pallas kernels: 39 us -> 86 us
  local copies, waits for them, and re-layouts: 9.25 us -> 0 us
    pallas_call x0 -> x1, Pallas kernels: none -> 48.8 us  [body(): pl.pallas_call(write_out, out_shape=tuple((jax.ShapeDtypeStruct(x.shape,...]
    unnamed x17 -> x0, local copies, waits for them, and re-layouts: 9.25 us -> none
    pallas_call x1, Pallas kernels: 39 us -> 37.2 us  [body(): pl.pallas_call(functools.partial(kernel, mesh.shape['inner'], mesh.shape[...]
where the time goes in v2:
time: 87.8 us; the launch traced here: 86.8 us
  Pallas kernels  86 us (98%)
    pallas_call x1, Pallas kernels, body(): pl.pallas_call(write_out, out_shape=tuple((jax.ShapeDtypeStruct(x.shape,...  48.8 us
    pallas_call x1, Pallas kernels, body(): pl.pallas_call(functools.partial(kernel, mesh.shape['inner'], mesh.shape[...  37.2 us

profile of v2, /device:TPU:0, one launch (start us, length us, event | category | flops | bytes accessed | tf_op | source)
XLA Modules:
  0.0 86.8 jit_solution(14276589497964778460)
XLA Ops:
  0.6 37.2 %shard_map.94 = (bf16[1,256,2048]{2,1,0:T(8,128)(2,1)}, bf16[1,256,512]{2,1,0:T(8,128)(2,1)}, bf16[1,256,512]{2,1,0:T(8,128)(2,1)}) custom-call(s32[1,1,3]{2,1,0:T(1,128)} %refs_0_.1, s32[1,1,8]{2,1,0:T(1,128)} %refs_1_.1, bf16[1,256,512]{2,1,0:T(8,128)(2,1)} %refs_2_.1, bf16[1,256,512]{2,1,0:T(8,128)(2,1)} %refs_3_.1, bf16[1,256,2048]{2,1,0:T(8,128)(2,1)} %refs_4_.1, ...), custom_call_target="tpu_custom_call" | custom-call | tf_op jit(solution)/shard_map/pallas_call | solution.py:289
  37.9 48.8 %shard_map.95 = (bf16[1,256,2048]{2,1,0:T(8,128)(2,1)}, bf16[1,256,512]{2,1,0:T(8,128)(2,1)}, bf16[1,256,512]{2,1,0:T(8,128)(2,1)}) custom-call(bf16[1,256,2048]{2,1,0:T(8,128)(2,1)} %get-tuple-element.6.refs_0_, bf16[1,256,512]{2,1,0:T(8,128)(2,1)} %get-tuple-element.7.refs_1_, bf16[1,256,512]{2,1,0:T(8,128)(2,1)} %get-tuple-element.8.refs_2_), custom_call_target="tpu_custom_call" | custom-call | tf_op jit(solution)/shard_map/pallas_call | solution.py:320
